TPU v7x, 32 devices: a whole 2x2x4 slice. The times are simulated.
32 devices in a mesh: band: 8 (over z, y), grid: 4 (over x, core).
Axes of the slice: x: 2, y: 2, z: 4, core: 2. Of those that a mesh axis runs over, the one named last changes fastest.
Arguments:
- orbitals: bfloat16 [512, 64, 4096], P('band', 'grid'), may hold values from -6 to 6
- picks: int32 [1], replicated, may hold values from 0 to 511
Outputs:
- exchange_vectors: bfloat16 [512, 64, 4096], P('band', 'grid')
- gram: float32 [512, 512], P('band')
All inputs are finite; a program needn't handle non-finite values.
Results may differ from a plain program's by a relative error of at most 0.00085.
Values may be sent and summed in bfloat16 or wider, within the bound.
A program may use at most 192 MiB of HBM per device.

v0:
```python
import math
import jax
import jax.numpy as jnp
from jax import lax
from jax.sharding import PartitionSpec as P

NG = 64
NPTS = 262144
KERNEL_SCALE = 128.0
HIGHEST = lax.Precision.HIGHEST


def spread(value, axis, source):
    kept = jnp.where(lax.axis_index(axis) == source, value, 0).astype(value.dtype)
    return lax.psum(kept, axis)


def cas_matrix(length):
    products = (
        jnp.arange(length, dtype=jnp.int32)[:, None]
        * jnp.arange(length, dtype=jnp.int32)[None, :]
        % length
    )
    angles = products.astype(jnp.float32) * (2.0 * math.pi / length)
    return jnp.cos(angles) + jnp.sin(angles)


def folded_squares(first, length):
    frequency = first + jnp.arange(length, dtype=jnp.int32)
    folded = jnp.minimum(frequency, NG - frequency).astype(jnp.float32)
    return folded * folded


def transform_planes(field, matrix):
    batch, planes, square = field.shape
    shaped = field.reshape(batch, planes, NG, NG)
    shaped = jnp.einsum("bxyz,zk->bxyk", shaped, matrix, precision=HIGHEST)
    shaped = jnp.einsum("bxyz,yk->bxkz", shaped, matrix, precision=HIGHEST)
    return shaped.reshape(batch, planes, square)


def solve_potential(density):
    matrix = cas_matrix(NG)
    slab_rows = NG // lax.axis_size("grid")
    squares_first = folded_squares(0, NG)
    squares_second = folded_squares(lax.axis_index("grid") * slab_rows, slab_rows)
    summed = (
        squares_first[:, None, None] + squares_second[None, :, None] + squares_first[None, None, :]
    )
    table = jnp.where(summed > 0, KERNEL_SCALE / NPTS / jnp.maximum(summed, 1.0), 0.0)
    table = table.reshape(NG, slab_rows * NG)
    spectral = transform_planes(density, matrix)
    moved = jnp.einsum(
        "bxq,xk->bkq",
        lax.all_to_all(spectral, "grid", split_axis=2, concat_axis=1, tiled=True),
        matrix,
        precision=HIGHEST,
    )
    moved = moved * table[None]
    moved = jnp.einsum("bxq,xk->bkq", moved, matrix, precision=HIGHEST)
    slabs = lax.all_to_all(moved, "grid", split_axis=1, concat_axis=2, tiled=True)
    return transform_planes(slabs, matrix)


def apply_exchange(values, partners, solver):
    accumulated = jnp.zeros(values.shape, jnp.float32)
    partner = partners[0]
    potential = solver(values * partner[None])
    accumulated = accumulated - potential * partner[None]
    return accumulated.astype(jnp.bfloat16)


def per_device(orbitals, picks):
    local_bands = orbitals.shape[0]
    target = picks[0]
    owner = target // local_bands
    offset = target % local_bands
    mine = lax.dynamic_index_in_dim(orbitals, offset, 0, keepdims=False)
    partners = [spread(mine, "band", owner).astype(jnp.float32)]
    vectors = apply_exchange(orbitals.astype(jnp.float32), partners, solve_potential)
    flat_orbitals = orbitals.reshape(local_bands, -1)
    flat_vectors = vectors.reshape(local_bands, -1)
    spread_orbitals, spread_vectors = (
        lax.all_to_all(flat_orbitals, "band", split_axis=1, concat_axis=0, tiled=True),
        lax.all_to_all(flat_vectors, "band", split_axis=1, concat_axis=0, tiled=True),
    )
    product = lax.dot_general(
        spread_orbitals,
        spread_vectors,
        (((1,), (1,)), ((), ())),
        preferred_element_type=jnp.float32,
    )
    partial_rows = lax.psum_scatter(product * (1.0 / NPTS), "band", scatter_dimension=0, tiled=True)
    gram = lax.psum(partial_rows, "grid")
    return (vectors, gram)


def solution(mesh):
    return jax.shard_map(
        per_device,
        mesh=mesh,
        in_specs=(P("band", "grid", None), P()),
        out_specs=(P("band", "grid", None), P("band", None)),
        check_vma=False,
    )
```

profile of v0, /device:TPU:0, one launch (start us, length us, event | category | flops | bytes accessed | tf_op | source)
XLA Modules:
  0.0 1356.4 jit_solution(10697332559528059427)
XLA Ops:
  7.9 1.6 select_bitcast_fusion
  9.5 74.8 %all-reduce.3.cloned.1.call-done = bf16[16,4096]{1,0:T(8,128)(2,1)} async-done(((bf16[16,4096]{1,0:T(8,128)(2,1)}), bf16[16,4096]{1,0:T(8,128)(2,1)}) %all-reduce.3.cloned.1.call-update) | async-done | bytes 131088 | tf_op jit(solution)/shard_map/psum | solution.py:15
  84.3 0.9 convert_element_type.50
  85.2 0.7 copy-done
  85.9 11.5 convert_multiply_fusion
  97.4 27.0 %reshape.119 = f32[64,16,64,64]{3,2,1,0:T(8,128)} reshape(f32[64,16,4096]{2,1,0:T(8,128)} %convert_multiply_fusion) | data formatting | bytes 33554432 | tf_op jit(solution)/shard_map/reshape | solution.py:36
  124.4 33.2 %fusion.15 = f32[64,16,64,64]{3,2,1,0:T(8,128)} fusion(f32[64,16,64,64]{3,2,1,0:T(8,128)} %reshape.119), kind=kOutput, calls=%fused_computation.25 | convolution fusion | flops 3221286912 | bytes 33554432 | tf_op jit(solution)/shard_map/bxyz,zk->bxyk/dot_general | solution.py:37
  157.6 37.2 %convolution_bitcast_fusion.1 = f32[64,16,64,64]{3,2,1,0:T(8,128)} fusion(f32[64,16,64,64]{3,2,1,0:T(8,128)} %fusion.15), kind=kOutput, calls=%fused_computation.10 | convolution fusion | flops 3221286912 | bytes 33554432 | tf_op jit(solution)/shard_map/bxyz,yk->bxkz/dot_general | solution.py:38
  194.9 33.0 %copy.39 = f32[64,16,64,64]{0,1,3,2:T(8,128)} copy(f32[64,16,64,64]{3,2,1,0:T(8,128)} %convolution_bitcast_fusion.1) | data formatting | bytes 33554432 | tf_op jit(solution)/shard_map/reshape | solution.py:39
  227.9 42.5 %reshape.130 = f32[4,1,1048576]{2,1,0:T(1,128)} reshape(f32[4096,16,64]{2,1,0:T(8,128)} %bitcast.70) | data formatting | bytes 33554432
  270.4 7.0 all-to-all-start
  277.4 0.1 broadcast_add_fusion
  277.5 0.2 add.104
  277.7 0.2 add.105
  277.9 0.1 add.107
  278.0 0.1 divide_select_fusion
  278.0 182.4 %all-to-all-done = f32[4,1,1048576]{2,1,0:T(1,128)} async-done(((f32[4,1,1048576]{2,1,0:T(1,128)}), f32[4,1,1048576]{2,1,0:T(1,128)}, u32[]{:S(2)}, u32[]{:S(2)}) %all-to-all-start) | async-done | bytes 16777248 | tf_op jit(solution)/shard_map/all_to_all | solution.py:55
  460.5 0.5 broadcast.113
  461.0 54.2 %reduce = f32[4,1048576]{1,0:T(4,128)} reduce(f32[4,1,1048576]{2,1,0:T(1,128)} %all-to-all-done, f32[]{:T(128)} %broadcast.113), dimensions={1}, to_apply=%all_to_all.50.reduce_sub_computation | reduce | bytes 33554436 | tf_op jit(solution)/shard_map/all_to_all | solution.py:55
  515.2 55.1 %reshape.131 = f32[4096,16,64]{2,1,0:T(8,128)} reshape(f32[4,1048576]{1,0:T(4,128)} %reduce) | data formatting | bytes 33554432
  570.3 26.6 %copy.40 = f32[64,16,4,1024]{3,2,1,0:T(4,128)} copy(f32[64,16,4,1024]{0,1,3,2:T(8,128)} %bitcast.69) | data formatting | bytes 33554432 | tf_op jit(solution)/shard_map/all_to_all | solution.py:55
  596.9 20.4 %copy.28 = f32[64,4,16,1024]{3,2,1,0:T(8,128)} copy(f32[64,4,16,1024]{3,1,2,0:T(4,128)} %bitcast.71) | data formatting | bytes 33554432 | tf_op jit(solution)/shard_map/all_to_all | solution.py:55
  617.3 21.9 %fusion.20 = f32[64,64,1024]{2,0,1:T(8,128)} fusion(f32[64,64,1024]{2,1,0:T(8,128)} %bitcast.73), kind=kOutput, calls=%fused_computation.30 | convolution fusion | flops 3221286912 | bytes 33554432 | tf_op jit(solution)/shard_map/bxq,xk->bkq/dot_general | solution.py:53
  639.3 22.2 %fusion.5 = f32[64,64,1024]{2,1,0:T(8,128)} fusion(f32[64,64,1024]{2,0,1:T(8,128)} %fusion.20, f32[64,1024]{1,0:T(8,128)S(1)} %divide_select_fusion), kind=kOutput, calls=%fused_computation.11 | convolution fusion | flops 3225481216 | bytes 33816576 | tf_op jit(solution)/shard_map/bxq,xk->bkq/dot_general | solution.py:60
  661.5 17.7 %copy.29 = f32[64,64,1024]{2,0,1:T(8,128)} copy(f32[64,64,1024]{2,1,0:T(8,128)} %fusion.5) | data formatting | bytes 33554432 | tf_op jit(solution)/shard_map/bxq,xk->bkq/transpose | solution.py:60
  679.2 7.2 all-to-all-start.1
  686.4 13.0 all_to_all.60
  699.4 11.2 copy.33
  710.7 158.8 %all-to-all-done.1 = f32[64,64,1024]{2,0,1:T(8,128)} async-done(((f32[64,64,1024]{2,0,1:T(8,128)}), f32[64,64,1024]{2,0,1:T(8,128)}, u32[]{:S(2)}, u32[]{:S(2)}) %all-to-all-start.1) | async-done | bytes 16777248 | tf_op jit(solution)/shard_map/all_to_all | solution.py:61
  869.4 5.0 all-to-all-start.3
  874.5 0.0 reduce-scatter.4.cloned.1.call-start
  874.6 20.9 %copy.50 = f32[64,4,16,1024]{3,1,2,0:T(4,128)} copy(f32[64,4,16,1024]{3,0,2,1:T(8,128)} %bitcast.14) | data formatting | bytes 33554432 | tf_op jit(solution)/shard_map/all_to_all | solution.py:61
  895.4 27.6 %reshape.121 = f32[64,16,64,64]{3,2,1,0:T(8,128)} reshape(f32[64,16,4,1024]{3,2,1,0:T(4,128)} %bitcast.72) | data formatting | bytes 33554432 | tf_op jit(solution)/shard_map/reshape | solution.py:36
  923.0 33.2 %fusion.13 = f32[64,16,64,64]{3,2,1,0:T(8,128)} fusion(f32[64,16,64,64]{3,2,1,0:T(8,128)} %reshape.121), kind=kOutput, calls=%fused_computation.23 | convolution fusion | flops 3221286912 | bytes 33554432 | tf_op jit(solution)/shard_map/bxyz,zk->bxyk/dot_general | solution.py:37
  956.3 37.3 %convolution_bitcast_fusion = f32[64,16,64,64]{3,2,1,0:T(8,128)} fusion(f32[64,16,64,64]{3,2,1,0:T(8,128)} %fusion.13), kind=kOutput, calls=%fused_computation.9 | convolution fusion | flops 3221286912 | bytes 33554432 | tf_op jit(solution)/shard_map/bxyz,yk->bxkz/dot_general | solution.py:38
  993.6 27.9 %reshape.123 = f32[64,8,8192]{2,1,0:T(8,128)} reshape(f32[64,16,64,64]{3,2,1,0:T(8,128)} %convolution_bitcast_fusion) | data formatting | bytes 33554432 | tf_op jit(solution)/shard_map/reshape | solution.py:39
  1021.5 17.6 %fusion.3 = bf16[64,8,8192]{2,0,1:T(8,128)(2,1)} fusion(f32[64,8,8192]{2,1,0:T(8,128)} %reshape.123, f32[8,8192]{1,0:T(8,128)S(1)} %mul.138), kind=kLoop, calls=%fused_computation.4 | loop fusion | flops 12582912 | bytes 25427968 | tf_op jit(solution)/shard_map/convert_element_type | solution.py:70
  1039.1 18.5 %all-to-all-done.3 = bf16[64,8,8192]{2,0,1:T(8,128)(2,1)} async-done(((bf16[64,8,8192]{2,0,1:T(8,128)(2,1)}), bf16[64,8,8192]{2,0,1:T(8,128)(2,1)}, u32[]{:S(2)}, u32[]{:S(2)}) %all-to-all-start.3) | async-done | bytes 8388640 | tf_op jit(solution)/shard_map/all_to_all | solution.py:84
  1057.6 186.9 %all_to_all.68 = bf16[64,8,8192]{2,0,1:T(8,128)(2,1)S(1)} all-to-all(bf16[64,8,8192]{2,0,1:T(8,128)(2,1)} %fusion.3), channel_id=1, replica_groups=mesh['band'=8,'grid'=4] {'band'}, dimensions={1} | all-to-all | bytes 16777216 | tf_op jit(solution)/shard_map/all_to_all | solution.py:85
  1244.4 7.1 fusion.9
  1251.5 1.3 copy.42
  1252.9 0.0 all-reduce.5.cloned.1.call-start
  1252.9 28.0 %reshape.122 = f32[64,16,4096]{2,1,0:T(8,128)} reshape(f32[64,16,64,64]{3,2,1,0:T(8,128)} %convolution_bitcast_fusion) | data formatting | bytes 33554432 | tf_op jit(solution)/shard_map/reshape | solution.py:39
  1281.0 33.7 %reduce-scatter.4.cloned.1.call-done = f32[64,512]{1,0:T(8,128)} async-done(((f32[512,512]{1,0:T(8,128)}), f32[64,512]{1,0:T(8,128)}) %reduce-scatter.4.cloned.1.call-update) | async-done | bytes 131088
  1314.6 1.7 copy.43
  1316.4 9.5 subtract_convert_fusion
  1325.9 22.1 %all-reduce.5.cloned.1.call-done = f32[64,512]{0,1:T(8,128)} async-done(((f32[64,512]{0,1:T(8,128)}), f32[64,512]{0,1:T(8,128)}) %all-reduce.5.cloned.1.call-update) | async-done | bytes 131088 | tf_op jit(solution)/shard_map/psum | solution.py:94
  1348.0 1.7 copy.34
  (13 shorter events, 0.2 us)
Async XLA Ops:
  7.2 77.1 %all-reduce.3.cloned.1.call-start = ((), (), s32[]{:S(2)}) async-start(), calls=%async_computation.5 | async-start | bytes 262144 | tf_op jit(solution)/shard_map/psum | solution.py:15
  85.2 0.7 copy-start
  270.4 190.0 %all-to-all-start = ((f32[4,1,1048576]{2,1,0:T(1,128)}), f32[4,1,1048576]{2,1,0:T(1,128)}, u32[]{:S(2)}, u32[]{:S(2)}) async-start(f32[4,1,1048576]{2,1,0:T(1,128)} %reshape.130), calls=%async_computation | async-start | bytes 33554432 | tf_op jit(solution)/shard_map/all_to_all | solution.py:55
  679.2 190.2 %all-to-all-start.1 = ((f32[64,64,1024]{2,0,1:T(8,128)}), f32[64,64,1024]{2,0,1:T(8,128)}, u32[]{:S(2)}, u32[]{:S(2)}) async-start(f32[64,64,1024]{2,0,1:T(8,128)} %copy.29), calls=%async_computation.1 | async-start | bytes 33554432 | tf_op jit(solution)/shard_map/all_to_all | solution.py:61
  699.4 175.1 %copy-start.2 = (bf16[16,4096]{1,0:T(8,128)(2,1)S(1)}, bf16[16,4096]{1,0:T(8,128)(2,1)}, u32[]{:S(2)}) copy-start(bf16[16,4096]{1,0:T(8,128)(2,1)} %all-reduce.3.cloned.1.call-done) | copy-start | bytes 393220
  869.4 188.2 %all-to-all-start.3 = ((bf16[64,8,8192]{2,0,1:T(8,128)(2,1)}), bf16[64,8,8192]{2,0,1:T(8,128)(2,1)}, u32[]{:S(2)}, u32[]{:S(2)}) async-start(bf16[64,8,8192]{2,0,1:T(8,128)(2,1)} %copy.33), calls=%async_computation.3 | async-start | bytes 16777216 | tf_op jit(solution)/shard_map/all_to_all | solution.py:84
  874.5 440.2 %reduce-scatter.4.cloned.1.call-start = ((), (), s32[]{:S(2)}) async-start(), calls=%async_computation.7 | async-start | bytes 1179648
  1252.9 63.5 %copy-start.1 = (f32[16,4096]{1,0:T(8,128)S(1)}, f32[16,4096]{1,0:T(8,128)}, u32[]{:S(2)}) copy-start(f32[16,4096]{1,0:T(8,128)} %copy-done) | copy-start | bytes 786436
  1252.9 95.1 %all-reduce.5.cloned.1.call-start = ((), (), s32[]{:S(2)}) async-start(), calls=%async_computation.6 | async-start | bytes 524288 | tf_op jit(solution)/shard_map/psum | solution.py:94
Sparse Core Ops, SparseCore 0:
  11.9 72.3 all-reduce.2
  1253.0 61.5 reduce-scatter.3
  1317.0 30.9 all-reduce.4
where the time goes:
time: 1370 us; the launch traced here: 1360 us
  waiting for transfers between devices  490 us (36%)
  local copies, waits for them, and re-layouts  358 us (26%)
  matrix products  192 us (14%)
  blocking collectives  187 us (14%)
  other arithmetic  95.4 us (7%)
  starting transfers between devices  19.3 us (1%)
  between operations  14.7 us (1%)
    all_to_all x1, blocking collectives, per_device(): lax.all_to_all(flat_vectors, 'band', split_axis=1, concat_axis=0, tiled=T...  187 us
    all_to_all x1, waiting for transfers between devices, solve_potential(): lax.all_to_all(spectral, 'grid', split_axis=2, concat_axis=1, tiled=True)  182 us
    all_to_all x1, waiting for transfers between devices, solve_potential(): lax.all_to_all(moved, 'grid', split_axis=1, concat_axis=2, tiled=True)  159 us
    unnamed x11, local copies, waits for them, and re-layouts  103 us
    reshape x3, local copies, waits for them, and re-layouts, transform_planes(): return shaped.reshape(batch, planes, square)  89 us
    psum x1, waiting for transfers between devices, spread(): return lax.psum(kept, axis)  74.8 us
    dot_general x2, matrix products, transform_planes(): shaped = jnp.einsum('bxyz,yk->bxkz', shaped, matrix, precision=HIGHEST)  74.5 us
    dot_general x2, matrix products, transform_planes(): shaped = jnp.einsum('bxyz,zk->bxyk', shaped, matrix, precision=HIGHEST)  66.5 us
  transfers between devices with their start and end apart: 6, of which 6 were waited for; matrix products, arithmetic and copies ran while one was open for 16% of the time, Pallas kernels for 0%

commit v1 on v0

--- a/solution.py
+++ b/solution.py
@@ -8,6 +8,12 @@
 NPTS = 262144
 KERNEL_SCALE = 128.0
 HIGHEST = lax.Precision.HIGHEST
+
+
+def swap_blocks(x, axis, split, join):
+    shards = jnp.split(x, lax.axis_size(axis), axis=split)
+    arrived = lax.all_to_all(jnp.stack(shards), axis, 0, 0)
+    return jnp.concatenate(arrived, axis=join)
 
 
 def spread(value, axis, source):
@@ -51,10 +57,7 @@
     table = table.reshape(NG, slab_rows * NG)
     spectral = transform_planes(density, matrix)
     moved = jnp.einsum(
-        "bxq,xk->bkq",
-        lax.all_to_all(spectral, "grid", split_axis=2, concat_axis=1, tiled=True),
-        matrix,
-        precision=HIGHEST,
+        "bxq,xk->bkq", swap_blocks(spectral, "grid", 2, 1), matrix, precision=HIGHEST
     )
     moved = moved * table[None]
     moved = jnp.einsum("bxq,xk->bkq", moved, matrix, precision=HIGHEST)

time: 1370 us -> 1190 us (0.87)
  local copies, waits for them, and re-layouts: 358 us -> 226 us
  other arithmetic: 95.4 us -> 47.2 us
    unnamed x11 -> x9, local copies, waits for them, and re-layouts: 103 us -> 5.47 us
    all_to_all x1 -> x0, other arithmetic: 54.2 us -> none  [solve_potential(): lax.all_to_all(spectral, 'grid', split_axis=2, concat_axis=1, tiled=True)]
    all_to_all x3 -> x1, local copies, waits for them, and re-layouts: 47.5 us -> 11.8 us  [swap_blocks(): arrived = lax.all_to_all(jnp.stack(shards), axis, 0, 0)]
  transfers between devices with their start and end apart: 6 -> 6, of which waited for: 6 -> 6; matrix products, arithmetic and copies ran while one was open for 16% -> 18% of each run, Pallas kernels for 0% -> 0%
where the time goes in v1:
time: 1190 us; the launch traced here: 1180 us
  waiting for transfers between devices  490 us (41%)
  local copies, waits for them, and re-layouts  226 us (19%)
  matrix products  192 us (16%)
  blocking collectives  187 us (16%)
  other arithmetic  47.2 us (4%)
  starting transfers between devices  19.8 us (2%)
  between operations  14.7 us (1%)
    all_to_all x1, blocking collectives, per_device(): lax.all_to_all(flat_vectors, 'band', split_axis=1, concat_axis=0, tiled=T...  187 us
    all_to_all x1, waiting for transfers between devices, swap_blocks(): arrived = lax.all_to_all(jnp.stack(shards), axis, 0, 0)  182 us
    all_to_all x1, waiting for transfers between devices, solve_potential(): lax.all_to_all(moved, 'grid', split_axis=1, concat_axis=2, tiled=True)  159 us
    reshape x3, local copies, waits for them, and re-layouts, transform_planes(): return shaped.reshape(batch, planes, square)  83.9 us
    psum x1, waiting for transfers between devices, spread(): return lax.psum(kept, axis)  74.8 us
    dot_general x2, matrix products, transform_planes(): shaped = jnp.einsum('bxyz,yk->bxkz', shaped, matrix, precision=HIGHEST)  74.6 us
    dot_general x2, matrix products, transform_planes(): shaped = jnp.einsum('bxyz,zk->bxyk', shaped, matrix, precision=HIGHEST)  66.5 us
    reshape x2, local copies, waits for them, and re-layouts, transform_planes(): shaped = field.reshape(batch, planes, NG, NG)  54.6 us
  transfers between devices with their start and end apart: 6, of which 6 were waited for; matrix products, arithmetic and copies ran while one was open for 18% of the time, Pallas kernels for 0%

profile of v1, /device:TPU:0, one launch (start us, length us, event | category | flops | bytes accessed | tf_op | source)
XLA Modules:
  0.0 1177.0 jit_solution(468874242345907901)
XLA Ops:
  7.2 0.0 all-reduce.3.cloned.1.call-start
  7.9 1.6 select_bitcast_fusion
  9.5 0.0 all-reduce.3.cloned.1.call-update
  9.5 74.8 %all-reduce.3.cloned.1.call-done = bf16[16,4096]{1,0:T(8,128)(2,1)} async-done(((bf16[16,4096]{1,0:T(8,128)(2,1)}), bf16[16,4096]{1,0:T(8,128)(2,1)}) %all-reduce.3.cloned.1.call-update) | async-done | bytes 131088 | tf_op jit(solution)/shard_map/psum | solution.py:21
  84.3 0.9 convert_element_type.50
  85.2 0.7 copy-done
  85.9 11.5 convert_multiply_fusion
  97.4 27.0 %reshape.125 = f32[64,16,64,64]{3,2,1,0:T(8,128)} reshape(f32[64,16,4096]{2,1,0:T(8,128)} %convert_multiply_fusion) | data formatting | bytes 33554432 | tf_op jit(solution)/shard_map/reshape | solution.py:42
  124.4 33.3 %fusion.15 = f32[64,16,64,64]{3,2,1,0:T(8,128)} fusion(f32[64,16,64,64]{3,2,1,0:T(8,128)} %reshape.125), kind=kOutput, calls=%fused_computation.30 | convolution fusion | flops 3221286912 | bytes 33554432 | tf_op jit(solution)/shard_map/bxyz,zk->bxyk/dot_general | solution.py:43
  157.7 37.2 %convolution_bitcast_fusion.1 = f32[64,16,64,64]{3,2,1,0:T(8,128)} fusion(f32[64,16,64,64]{3,2,1,0:T(8,128)} %fusion.15), kind=kOutput, calls=%fused_computation.11 | convolution fusion | flops 3221286912 | bytes 33554432 | tf_op jit(solution)/shard_map/bxyz,yk->bxkz/dot_general | solution.py:44
  194.9 27.9 %reshape.126 = f32[64,16,4096]{2,1,0:T(8,128)} reshape(f32[64,16,64,64]{3,2,1,0:T(8,128)} %convolution_bitcast_fusion.1) | data formatting | bytes 33554432 | tf_op jit(solution)/shard_map/reshape | solution.py:45
  222.8 6.7 slice_bitcast_fusion.3
  229.6 6.0 pad_maximum_fusion
  235.6 7.5 all-to-all-start
  243.1 0.1 broadcast_add_fusion
  243.2 0.2 add.104
  243.4 0.2 add.105
  243.6 0.1 add.107
  243.7 0.1 divide_select_fusion
  243.7 182.4 %all-to-all-done = f32[4,64,16,1024]{3,2,1,0:T(8,128)} async-done(((f32[4,64,16,1024]{3,2,1,0:T(8,128)}), f32[4,64,16,1024]{3,2,1,0:T(8,128)}, u32[]{:S(2)}, u32[]{:S(2)}) %all-to-all-start) | async-done | bytes 16777248 | tf_op jit(solution)/shard_map/all_to_all | solution.py:15
  426.2 11.8 %copy.21 = f32[4,64,16,1024]{3,2,0,1:T(8,128)} copy(f32[4,64,16,1024]{3,2,1,0:T(8,128)} %all-to-all-done) | data formatting | bytes 33554432 | tf_op jit(solution)/shard_map/all_to_all | solution.py:15
  438.0 21.8 %fusion.20 = f32[64,64,1024]{2,0,1:T(8,128)} fusion(f32[64,64,1024]{2,1,0:T(8,128)} %bitcast.77), kind=kOutput, calls=%fused_computation.35 | convolution fusion | flops 3221286912 | bytes 33554432 | tf_op jit(solution)/shard_map/bxq,xk->bkq/dot_general | solution.py:59
  459.7 22.4 %fusion.5 = f32[64,64,1024]{2,1,0:T(8,128)} fusion(f32[64,64,1024]{2,0,1:T(8,128)} %fusion.20, f32[64,1024]{1,0:T(8,128)S(1)} %divide_select_fusion), kind=kOutput, calls=%fused_computation.12 | convolution fusion | flops 3225481216 | bytes 33816576 | tf_op jit(solution)/shard_map/bxq,xk->bkq/dot_general | solution.py:63
  482.1 17.7 %copy.22 = f32[64,64,1024]{2,0,1:T(8,128)} copy(f32[64,64,1024]{2,1,0:T(8,128)} %fusion.5) | data formatting | bytes 33554432 | tf_op jit(solution)/shard_map/bxq,xk->bkq/transpose | solution.py:63
  499.8 7.2 all-to-all-start.1
  507.0 13.0 %all_to_all.47 = bf16[64,8,8192]{2,1,0:T(8,128)(2,1)} reshape(bf16[64,16,4096]{2,1,0:T(8,128)(2,1)} %param.2) | data formatting | bytes 16777216 | tf_op jit(solution)/shard_map/all_to_all | solution.py:87
  520.1 11.2 copy.26
  531.3 158.8 %all-to-all-done.1 = f32[64,64,1024]{2,0,1:T(8,128)} async-done(((f32[64,64,1024]{2,0,1:T(8,128)}), f32[64,64,1024]{2,0,1:T(8,128)}, u32[]{:S(2)}, u32[]{:S(2)}) %all-to-all-start.1) | async-done | bytes 16777248 | tf_op jit(solution)/shard_map/all_to_all | solution.py:64
  690.1 5.0 all-to-all-start.3
  695.1 0.0 reduce-scatter.4.cloned.1.call-start
  695.2 20.9 %copy.41 = f32[64,4,16,1024]{3,1,2,0:T(4,128)} copy(f32[64,4,16,1024]{3,0,2,1:T(8,128)} %bitcast.16) | data formatting | bytes 33554432 | tf_op jit(solution)/shard_map/all_to_all | solution.py:64
  716.1 27.6 %reshape.129 = f32[64,16,64,64]{3,2,1,0:T(8,128)} reshape(f32[64,16,4,1024]{3,2,1,0:T(4,128)} %bitcast.76) | data formatting | bytes 33554432 | tf_op jit(solution)/shard_map/reshape | solution.py:42
  743.7 33.3 %fusion.13 = f32[64,16,64,64]{3,2,1,0:T(8,128)} fusion(f32[64,16,64,64]{3,2,1,0:T(8,128)} %reshape.129), kind=kOutput, calls=%fused_computation.28 | convolution fusion | flops 3221286912 | bytes 33554432 | tf_op jit(solution)/shard_map/bxyz,zk->bxyk/dot_general | solution.py:43
  776.9 37.3 %convolution_bitcast_fusion = f32[64,16,64,64]{3,2,1,0:T(8,128)} fusion(f32[64,16,64,64]{3,2,1,0:T(8,128)} %fusion.13), kind=kOutput, calls=%fused_computation.10 | convolution fusion | flops 3221286912 | bytes 33554432 | tf_op jit(solution)/shard_map/bxyz,yk->bxkz/dot_general | solution.py:44
  814.2 27.9 %reshape.131 = f32[64,8,8192]{2,1,0:T(8,128)} reshape(f32[64,16,64,64]{3,2,1,0:T(8,128)} %convolution_bitcast_fusion) | data formatting | bytes 33554432 | tf_op jit(solution)/shard_map/reshape | solution.py:45
  842.2 17.6 %fusion.3 = bf16[64,8,8192]{2,0,1:T(8,128)(2,1)} fusion(f32[64,8,8192]{2,1,0:T(8,128)} %reshape.131, f32[8,8192]{1,0:T(8,128)S(1)} %mul.138), kind=kLoop, calls=%fused_computation.5 | loop fusion | flops 12582912 | bytes 25427968 | tf_op jit(solution)/shard_map/convert_element_type | solution.py:73
  859.7 18.5 %all-to-all-done.3 = bf16[64,8,8192]{2,0,1:T(8,128)(2,1)} async-done(((bf16[64,8,8192]{2,0,1:T(8,128)(2,1)}), bf16[64,8,8192]{2,0,1:T(8,128)(2,1)}, u32[]{:S(2)}, u32[]{:S(2)}) %all-to-all-start.3) | async-done | bytes 8388640 | tf_op jit(solution)/shard_map/all_to_all | solution.py:87
  878.2 186.9 %all_to_all.55 = bf16[64,8,8192]{2,0,1:T(8,128)(2,1)S(1)} all-to-all(bf16[64,8,8192]{2,0,1:T(8,128)(2,1)} %fusion.3), channel_id=1, replica_groups=mesh['band'=8,'grid'=4] {'band'}, dimensions={1} | all-to-all | bytes 16777216 | tf_op jit(solution)/shard_map/all_to_all | solution.py:88
  1065.1 7.1 fusion.9
  1072.2 1.3 copy.33
  1073.5 0.0 reduce-scatter.4.cloned.1.call-update
  1073.5 0.0 all-reduce.5.cloned.1.call-start
  1073.6 28.0 %reshape.130 = f32[64,16,4096]{2,1,0:T(8,128)} reshape(f32[64,16,64,64]{3,2,1,0:T(8,128)} %convolution_bitcast_fusion) | data formatting | bytes 33554432 | tf_op jit(solution)/shard_map/reshape | solution.py:45
  1101.6 33.6 %reduce-scatter.4.cloned.1.call-done = f32[64,512]{1,0:T(8,128)} async-done(((f32[512,512]{1,0:T(8,128)}), f32[64,512]{1,0:T(8,128)}) %reduce-scatter.4.cloned.1.call-update) | async-done | bytes 131088
  1135.2 1.7 copy.34
  1137.0 9.5 subtract_convert_fusion
  1146.5 22.1 %all-reduce.5.cloned.1.call-done = f32[64,512]{0,1:T(8,128)} async-done(((f32[64,512]{0,1:T(8,128)}), f32[64,512]{0,1:T(8,128)}) %all-reduce.5.cloned.1.call-update) | async-done | bytes 131088 | tf_op jit(solution)/shard_map/psum | solution.py:97
  1168.6 1.7 copy.27
  (10 shorter events, 0.1 us)
Async XLA Ops:
  7.2 77.1 %all-reduce.3.cloned.1.call-start = ((), (), s32[]{:S(2)}) async-start(), calls=%async_computation.5 | async-start | bytes 262144 | tf_op jit(solution)/shard_map/psum | solution.py:21
  85.2 0.7 copy-start
  235.6 190.6 %all-to-all-start = ((f32[4,64,16,1024]{3,2,1,0:T(8,128)}), f32[4,64,16,1024]{3,2,1,0:T(8,128)}, u32[]{:S(2)}, u32[]{:S(2)}) async-start(f32[4,64,16,1024]{3,2,1,0:T(8,128)} %pad_maximum_fusion), calls=%async_computation | async-start | bytes 33554432 | tf_op jit(solution)/shard_map/all_to_all | solution.py:15
  499.8 190.2 %all-to-all-start.1 = ((f32[64,64,1024]{2,0,1:T(8,128)}), f32[64,64,1024]{2,0,1:T(8,128)}, u32[]{:S(2)}, u32[]{:S(2)}) async-start(f32[64,64,1024]{2,0,1:T(8,128)} %copy.22), calls=%async_computation.1 | async-start | bytes 33554432 | tf_op jit(solution)/shard_map/all_to_all | solution.py:64
  520.1 175.1 %copy-start.2 = (bf16[16,4096]{1,0:T(8,128)(2,1)S(1)}, bf16[16,4096]{1,0:T(8,128)(2,1)}, u32[]{:S(2)}) copy-start(bf16[16,4096]{1,0:T(8,128)(2,1)} %all-reduce.3.cloned.1.call-done) | copy-start | bytes 393220
  690.1 188.2 %all-to-all-start.3 = ((bf16[64,8,8192]{2,0,1:T(8,128)(2,1)}), bf16[64,8,8192]{2,0,1:T(8,128)(2,1)}, u32[]{:S(2)}, u32[]{:S(2)}) async-start(bf16[64,8,8192]{2,0,1:T(8,128)(2,1)} %copy.26), calls=%async_computation.3 | async-start | bytes 16777216 | tf_op jit(solution)/shard_map/all_to_all | solution.py:87
  695.1 440.1 %reduce-scatter.4.cloned.1.call-start = ((), (), s32[]{:S(2)}) async-start(), calls=%async_computation.7 | async-start | bytes 1179648
  1073.5 63.5 %copy-start.1 = (f32[16,4096]{1,0:T(8,128)S(1)}, f32[16,4096]{1,0:T(8,128)}, u32[]{:S(2)}) copy-start(f32[16,4096]{1,0:T(8,128)} %copy-done) | copy-start | bytes 786436
  1073.5 95.1 %all-reduce.5.cloned.1.call-start = ((), (), s32[]{:S(2)}) async-start(), calls=%async_computation.6 | async-start | bytes 524288 | tf_op jit(solution)/shard_map/psum | solution.py:97
Sparse Core Ops, SparseCore 0:
  11.9 72.3 all-reduce.2
  1073.6 61.5 reduce-scatter.3
  1137.5 30.9 all-reduce.4
